TPU v7x, 32 devices: a whole 2x2x4 slice. The times are simulated.
32 devices in a mesh: groups: 2 (over x), rows: 2 (over core), tensor: 8 (over z, y).
Axes of the slice: x: 2, y: 2, z: 4, core: 2. Of those that a mesh axis runs over, the one named last changes fastest.
Arguments:
- features: bfloat16 [6144, 8192], P(('groups', 'rows'), 'tensor'), parts along dimension 0, may hold values from -6 to 6
- qkv_weight: bfloat16 [8192, 10240], P(None, 'tensor'), may hold values from -0.0625 to 0.0625
- adapter_ids: int32 [6144, 1], P(('groups', 'rows')), parts along dimension 0, may hold values from 0 to 31; in each aligned block of 192 rows (0 to 191, 192 to 383, ...) at most 12 rows name the same one
- owner_slot: int32 [32], replicated, may hold values from 0 to 31, each once
- shrink_panels: bfloat16 [32, 8192, 64], P(('rows', 'tensor')), may hold values from -0.0625 to 0.0625
- expand_panels: bfloat16 [32, 64, 10240], P(('rows', 'tensor')), may hold values from -0.75 to 0.75
Outputs:
- projected: bfloat16 [6144, 10240], P(('groups', 'rows'), 'tensor'), parts along dimension 0
There are 2 independent parts, one for each index of `groups`. A program takes and returns all parts, laid end to end along the dimension named above; an argument that names none is the same for every part. Nothing has to cross between parts.
Inputs may be any that keep to these rules, and one draw needn't show every extreme that they name: `adapter_ids`: each row names one adapter. In each aligned block of 192 rows no adapter is named by more than 12 rows, and in some block one adapter is named by exactly 12 rows. A permutation: the panels of adapter k stand at index owner_slot[k] of shrink_panels and expand_panels.
All inputs are finite; a program needn't handle non-finite values.
Results may differ from a plain program's by a relative error of at most 0.005.
Values may be sent and summed in bfloat16 or wider, within the bound.
A program may use at most 192 MiB of HBM per device.

v0:
```python
import jax
import jax.numpy as jnp
from jax import lax
from jax.sharding import PartitionSpec as P


def slot_of(row_ids, owner_slot):
    count = owner_slot.shape[0]
    match = row_ids[:, None] == jnp.arange(count, dtype=jnp.int32)[None, :]
    return jnp.sum(jnp.where(match, owner_slot[None, :], 0), axis=1)


def on_device(features, qkv_weight, adapter_ids, owner_slot, shrink_panels, expand_panels):
    tok_rows = features.shape[0]
    width = qkv_weight.shape[0]
    full_columns = expand_panels.shape[2]
    tensor_count = lax.axis_size("tensor")
    block_rows = tok_rows // tensor_count
    adapter_count = owner_slot.shape[0]
    per_device = shrink_panels.shape[0]
    device_count = adapter_count // per_device
    most = max(2, 2 * tok_rows // (tensor_count * adapter_count))
    tensor_pos = lax.axis_index("tensor")
    start_row = tensor_pos * block_rows
    piece = lax.all_gather(features, "tensor", axis=1, tiled=True)
    total = jnp.dot(piece, qkv_weight, preferred_element_type=jnp.float32)
    picked = lax.dynamic_slice_in_dim(piece, start_row, block_rows, 0)
    my_rows = picked
    base, my_rows = (total, my_rows)
    my_ids = lax.dynamic_slice_in_dim(adapter_ids[:, 0], start_row, block_rows, 0)
    my_slot = slot_of(my_ids, owner_slot)
    slot_match = (my_slot[:, None] == jnp.arange(adapter_count, dtype=jnp.int32)[None, :]).astype(
        jnp.int32
    )
    earlier = jnp.cumsum(slot_match, axis=0) - slot_match
    rank = jnp.sum(earlier * slot_match, axis=1)
    position = my_slot * most + rank
    placer = (
        jnp.arange(adapter_count * most, dtype=jnp.int32)[:, None] == position[None, :]
    ).astype(jnp.bfloat16)
    outgoing = jnp.dot(placer, my_rows, preferred_element_type=jnp.float32).astype(jnp.bfloat16)
    outgoing = outgoing.reshape(device_count, per_device, most, width)
    shrunk = jnp.einsum(
        "sjmd,jdr->sjmr",
        lax.all_to_all(outgoing, ("rows", "tensor"), split_axis=0, concat_axis=0, tiled=True),
        shrink_panels,
        preferred_element_type=jnp.float32,
    ).astype(jnp.bfloat16)
    reply = jnp.einsum(
        "sjmr,jre->sjme", shrunk, expand_panels, preferred_element_type=jnp.float32
    ).astype(jnp.bfloat16)
    back = lax.all_to_all(
        reply, ("rows", "tensor"), split_axis=0, concat_axis=0, tiled=True
    ).reshape(adapter_count * most, full_columns)
    delta_rows = jnp.dot(placer.T, back, preferred_element_type=jnp.float32).astype(jnp.bfloat16)
    delta = lax.all_to_all(delta_rows, "tensor", split_axis=1, concat_axis=0, tiled=True)
    return (base + delta.astype(jnp.float32)).astype(jnp.bfloat16)


def solution(mesh):
    return jax.shard_map(
        on_device,
        mesh=mesh,
        in_specs=(
            P(("groups", "rows"), "tensor"),
            P(None, "tensor"),
            P(("groups", "rows"), None),
            P(),
            P(("rows", "tensor"), None, None),
            P(("rows", "tensor"), None, None),
        ),
        out_specs=P(("groups", "rows"), "tensor"),
        check_vma=False,
    )
```

profile of v0, /device:TPU:0, one launch (start us, length us, event | category | flops | bytes accessed | tf_op | source)
XLA Modules:
  0.0 1041.7 jit_solution(13207671742248062491)
XLA Ops:
  6.5 0.0 copy-start
  6.5 0.0 all-gather.2.cloned.1.call-start
  6.5 0.7 all-gather.2.cloned.1.call-update
  7.3 0.8 constant_dynamic-slice_fusion
  8.1 0.7 select_reduce_fusion
  8.9 0.6 reduce-window.6
  9.4 0.2 slice_reduce_fusion
  9.7 0.1 bitcast_bitcast_fusion
  9.8 482.3 %all-gather.2.cloned.1.call-done = bf16[1536,8192]{1,0:T(8,128)(2,1)} async-done(((bf16[1536,1024]{1,0:T(8,128)(2,1)}), bf16[1536,8192]{1,0:T(8,128)(2,1)}) %all-gather.2.cloned.1.call-update) | async-done | bytes 25165840 | tf_op jit(solution)/shard_map/all_gather | solution.py:25
  492.1 6.3 convolution_convert_fusion.2
  498.3 8.6 reshape.34
  506.9 11.9 %copy.21 = bf16[16,2,12,8192]{3,1,2,0:T(2,128)(2,1)S(1)} copy(bf16[16,2,12,8192]{3,2,1,0:T(8,128)(2,1)} %reshape.34) | data formatting | bytes 12582912 | tf_op jit(solution)/shard_map/reshape | solution.py:42
  518.8 0.0 copy-start.2
  518.8 144.0 %all_to_all.23 = bf16[16,2,12,8192]{3,1,2,0:T(2,128)(2,1)S(1)} all-to-all(bf16[16,2,12,8192]{3,1,2,0:T(2,128)(2,1)S(1)} %copy.21), channel_id=1, replica_groups=mesh['groups'=2,'rows'=2,'tensor'=8] {'rows','tensor'}, dimensions={0} | all-to-all | bytes 12582912 | tf_op jit(solution)/shard_map/all_to_all | solution.py:45
  662.8 0.0 copy-done.2
  662.8 3.6 fusion.12
  666.5 0.0 copy-done
  666.5 2.2 fusion
  668.7 22.8 %copy.24 = bf16[16,2,12,10240]{3,1,2,0:T(2,128)(2,1)S(1)} copy(bf16[16,2,12,10240]{3,0,2,1:T(8,128)(2,1)S(1)} %fusion) | data formatting | bytes 15728640 | tf_op jit(solution)/shard_map/convert_element_type | solution.py:51
  691.5 176.5 %all_to_all.24 = bf16[16,2,12,10240]{3,1,2,0:T(2,128)(2,1)} all-to-all(bf16[16,2,12,10240]{3,1,2,0:T(2,128)(2,1)S(1)} %copy.24), channel_id=1, replica_groups=mesh['groups'=2,'rows'=2,'tensor'=8] {'rows','tensor'}, dimensions={0} | all-to-all | bytes 15728640 | tf_op jit(solution)/shard_map/all_to_all | solution.py:52
  868.0 10.9 %copy.25 = bf16[16,2,12,10240]{3,2,1,0:T(8,128)(2,1)} copy(bf16[16,2,12,10240]{3,1,2,0:T(2,128)(2,1)} %all_to_all.24) | data formatting | bytes 15728640 | tf_op jit(solution)/shard_map/all_to_all | solution.py:52
  878.9 12.9 %reshape.35 = bf16[384,10240]{1,0:T(8,128)(2,1)} reshape(bf16[16,2,12,10240]{3,2,1,0:T(8,128)(2,1)} %copy.25) | data formatting | bytes 15728640 | tf_op jit(solution)/shard_map/reshape | solution.py:54
  891.8 5.5 convolution_convert_fusion.1
  897.3 0.3 copy.43
  897.6 90.0 %all_to_all.25 = bf16[192,8,1280]{2,0,1:T(8,128)(2,1)S(1)} all-to-all(bf16[192,8,1280]{2,0,1:T(8,128)(2,1)S(1)} %bitcast.42), channel_id=1, replica_groups=mesh['groups'=2,'rows'=2,'tensor'=8] {'tensor'}, dimensions={1} | all-to-all | bytes 7864320 | tf_op jit(solution)/shard_map/all_to_all | solution.py:56
  987.5 3.8 convert_element_type.47
  991.4 0.0 copy-start.1
  991.4 43.5 %fusion.3 = bf16[1536,1280]{1,0:T(8,128)(2,1)} fusion(f32[1536,1280]{1,0:T(8,128)} %bitcast.43, bf16[1536,8192]{1,0:T(8,128)(2,1)} %all-gather.2.cloned.1.call-done, bf16[8192,1280]{1,0:T(8,128)(2,1)} %param.7), kind=kOutput, calls=%fused_computation.7 | convolution fusion | flops 32216186880 | bytes 57933824 | tf_op jit(solution)/shard_map/dot_general | solution.py:26
  1034.9 0.0 copy-done.1
  (6 shorter events, 0.1 us)
Async XLA Ops:
  6.5 659.9 %copy-start = (bf16[2,64,10240]{2,1,0:T(8,128)(2,1)S(1)}, bf16[2,64,10240]{2,1,0:T(8,128)(2,1)}, u32[]{:S(2)}) copy-start(bf16[2,64,10240]{2,1,0:T(8,128)(2,1)} %param.11) | copy-start | bytes 7864324
  6.5 485.5 %all-gather.2.cloned.1.call-start = ((), (), s32[]{:S(2)}) async-start(), calls=%async_computation.3 | async-start | bytes 28311552 | tf_op jit(solution)/shard_map/all_gather | solution.py:25
  518.8 144.0 %copy-start.2 = (bf16[2,8192,64]{1,2,0:T(8,128)(2,1)S(1)}, bf16[2,8192,64]{1,2,0:T(8,128)(2,1)}, u32[]{:S(2)}) copy-start(bf16[2,8192,64]{1,2,0:T(8,128)(2,1)} %param.10) | copy-start | bytes 6291460
  991.4 43.5 %copy-start.1 = (bf16[2,64,10240]{2,1,0:T(8,128)(2,1)S(1)}, bf16[2,64,10240]{2,1,0:T(8,128)(2,1)}, u32[]{:S(2)}) copy-start(bf16[2,64,10240]{2,1,0:T(8,128)(2,1)} %param.11) | copy-start | bytes 7864324
Sparse Core Ops, SparseCore 0:
  8.9 483.1 all-gather.1
where the time goes:
time: 1040 us
  waiting for transfers between devices  483 us (46%)
  blocking collectives  411 us (40%)
  local copies, waits for them, and re-layouts  68.3 us (7%)
  matrix products  61.1 us (6%)
  between operations  13.5 us (1%)
    all_gather x1, waiting for transfers between devices, on_device(): piece = lax.all_gather(features, 'tensor', axis=1, tiled=True)  482 us
    all_to_all x1, blocking collectives, on_device(): lax.all_to_all(reply, ('rows', 'tensor'), split_axis=0, concat_axis=0, ti...  177 us
    all_to_all x1, blocking collectives, on_device(): lax.all_to_all(outgoing, ('rows', 'tensor'), split_axis=0, concat_axis=0,...  144 us
    all_to_all x1, blocking collectives, on_device(): lax.all_to_all(delta_rows, 'tensor', split_axis=1, concat_axis=0, tiled=T...  90 us
    dot_general x1, matrix products, on_device(): total = jnp.dot(piece, qkv_weight, preferred_element_type=jnp.float32)  43.5 us
    convert_element_type x1, local copies, waits for them, and re-layouts, on_device(): reply = jnp.einsum('sjmr,jre->sjme', shrunk, expand_panels, preferred_ele...  22.8 us
  transfers between devices with their start and end apart: 1, of which 1 were waited for; matrix products, arithmetic and copies ran while one was open for 0% of the time, Pallas kernels for 0%

commit v1 on v0

v1 whole, which is shorter than its diff:
```python
import functools

import jax
import jax.numpy as jnp
from jax import lax
from jax.experimental import pallas as pl
from jax.experimental.pallas import tpu as pltpu
from jax.sharding import PartitionSpec as P

CHUNKS = 8
LAG = 2


def slot_of(row_ids, owner_slot):
    count = owner_slot.shape[0]
    match = row_ids[:, None] == jnp.arange(count, dtype=jnp.int32)[None, :]
    return jnp.sum(jnp.where(match, owner_slot[None, :], 0), axis=1)


def gather_kernel(
    Z, Y, CH, NB,
    x_ref, w_ref, sh_ref, base_ref, low_ref,
    g, w, ws, acc, low,
    own_sem, w_sem, ws_sem, ws_send, ws_recv,
    up_send, dn_send, z_recv, ub_send, db_send, b_recv, y_send, y_recv, out_sem,
):
    NC = x_ref.shape[0] // CH
    DK = x_ref.shape[1]
    T = Z * Y
    NA = CH - NB
    t = lax.axis_index("tensor")
    r = lax.axis_index("rows")
    z, y = t // Y, lax.rem(t, Y)
    has_up, has_dn = z < Z - 1, z > 0
    up, dn, side = {"tensor": t + Y}, {"tensor": t - Y}, {"tensor": z * Y + (1 - y)}
    twin = {"rows": 1 - r}

    barrier = pltpu.get_barrier_semaphore()

    @pl.when(has_up)
    def _():
        pl.semaphore_signal(barrier, inc=1, device_id=up)

    @pl.when(has_dn)
    def _():
        pl.semaphore_signal(barrier, inc=1, device_id=dn)

    if Y == 2:
        pl.semaphore_signal(barrier, inc=1, device_id=side)
    pl.semaphore_signal(barrier, inc=1, device_id=twin)
    pl.semaphore_wait(barrier, has_up.astype(jnp.int32) + has_dn.astype(jnp.int32) + Y)

    own_copy = pltpu.make_async_copy(x_ref, g.at[t], own_sem)
    w_copy = pltpu.make_async_copy(w_ref, w, w_sem)
    ws_cols = pl.ds(pl.multiple_of(r * 128, 128), 128)
    ws_copy = pltpu.make_async_copy(sh_ref, ws.at[:, ws_cols], ws_sem)
    ws_remote = pltpu.make_async_remote_copy(
        src_ref=sh_ref, dst_ref=ws.at[:, ws_cols], send_sem=ws_send, recv_sem=ws_recv, device_id=twin,
    )
    twin_cols = pl.ds(pl.multiple_of((1 - r) * 128, 128), 128)
    ws_in = pltpu.make_async_remote_copy(
        src_ref=sh_ref, dst_ref=ws.at[:, twin_cols], send_sem=ws_send, recv_sem=ws_recv, device_id=twin,
    )

    def rows_all(c):
        return pl.ds(pl.multiple_of(c * CH, CH), CH)

    def rows_a(c):
        return pl.ds(pl.multiple_of(c * CH, 16), NA)

    def rows_b(c):
        return pl.ds(pl.multiple_of(c * CH + NA, 16), NB)

    def place(zs, ys, rows):
        return g.at[zs * Y + ys, rows]

    def own_src(c):
        return x_ref.at[rows_all(c)]

    def along(c, zs, src, upward):
        return pltpu.make_async_remote_copy(
            src_ref=src, dst_ref=place(zs, y, rows_all(c)),
            send_sem=(up_send if upward else dn_send).at[c, zs], recv_sem=z_recv.at[c, zs],
            device_id=up if upward else dn,
        )

    def along_b(c, zs, upward):
        ref = place(zs, 1 - y, rows_b(c))
        return pltpu.make_async_remote_copy(
            src_ref=ref, dst_ref=ref,
            send_sem=(ub_send if upward else db_send).at[c, zs], recv_sem=b_recv.at[c, zs],
            device_id=up if upward else dn,
        )

    def across_own(c):
        return pltpu.make_async_remote_copy(
            src_ref=own_src(c), dst_ref=place(z, y, rows_all(c)),
            send_sem=y_send.at[c, z], recv_sem=y_recv.at[c, z], device_id=side,
        )

    def across(c, zs):
        ref = place(zs, y, rows_a(c))
        return pltpu.make_async_remote_copy(
            src_ref=ref, dst_ref=ref,
            send_sem=y_send.at[c, zs], recv_sem=y_recv.at[c, zs], device_id=side,
        )

    def wait_into(ref, sem):
        pltpu.make_async_remote_copy(
            src_ref=ref, dst_ref=ref, send_sem=sem, recv_sem=sem, device_id=twin,
        ).wait_recv()

    def when_chunk(c, cond=True):
        return pl.when((c >= 0) & (c < NC) & cond)

    def out_copies(c):
        slot = lax.rem(c, 2)
        return (
            pltpu.make_async_copy(acc.at[slot], base_ref.at[rows_all(c)], out_sem.at[slot, 0]),
            pltpu.make_async_copy(low.at[slot], low_ref.at[rows_all(c)], out_sem.at[slot, 1]),
        )

    def compute(c):
        slot = lax.rem(c, 2)

        @pl.when(c >= 2)
        def _():
            for copy in out_copies(c - 2):
                copy.wait()

        def one(s, sums):
            rows = g[s, rows_all(c), :]
            depth = pl.ds(pl.multiple_of(s * DK, DK), DK)
            part = jnp.dot(rows, w[depth, :], preferred_element_type=jnp.float32)
            first = s == 0
            acc[slot] = jnp.where(first, part, acc[slot] + part)
            return sums + jnp.dot(rows, ws[depth, :], preferred_element_type=jnp.float32)

        sums = lax.fori_loop(0, T, one, jnp.zeros((CH, 256), jnp.float32))
        low[slot] = sums.astype(low.dtype)
        for copy in out_copies(c):
            copy.start()

    def step(k, carry):
        @pl.when(k < NC)
        def _():
            @pl.when(has_up)
            def _():
                along(k, z, own_src(k), True).start()

            @pl.when(has_dn)
            def _():
                along(k, z, own_src(k), False).start()

            if Y == 2:
                across_own(k).start()

        @pl.when(k == 0)
        def _():
            ws_remote.start()
            ws_copy.start()
            own_copy.start()
            w_copy.start()

        if Y == 2:
            c1 = k - LAG

            @when_chunk(c1)
            def _():
                wait_into(place(z, 1 - y, rows_all(c1)), y_recv.at[c1, z])

                @pl.when(has_up)
                def _():
                    along_b(c1, z, True).start()

                @pl.when(has_dn)
                def _():
                    along_b(c1, z, False).start()

        for d in range(1, Z):
            for upward in (True, False):
                zs = z - d if upward else z + d
                here = zs >= 0 if upward else zs < Z
                more = has_up if upward else has_dn
                c = k - LAG * d

                @when_chunk(c, here)
                def _(c=c, zs=zs, upward=upward, more=more):
                    ref = place(zs, y, rows_all(c))
                    wait_into(ref, z_recv.at[c, zs])

                    @pl.when(more)
                    def _():
                        along(c, zs, ref, upward).start()

                    if Y == 2:
                        across(c, zs).start()

                if Y == 2:
                    cb = k - LAG * (d + 1)

                    @when_chunk(cb, here)
                    def _(c=cb, zs=zs, upward=upward, more=more):
                        wait_into(place(zs, 1 - y, rows_b(c)), b_recv.at[c, zs])

                        @pl.when(more)
                        def _():
                            along_b(c, zs, upward).start()

        @pl.when(k == LAG * Z)
        def _():
            own_copy.wait()
            w_copy.wait()
            ws_copy.wait()
            ws_in.wait_recv()

        cc = k - LAG * Z

        @when_chunk(cc)
        def _():
            if Y == 2:
                for zs in range(Z):
                    @pl.when(zs != z)
                    def _(zs=zs):
                        wait_into(place(zs, 1 - y, rows_a(cc)), y_recv.at[cc, zs])
            compute(cc)

        return carry

    lax.fori_loop(0, NC + LAG * Z, step, 0)

    for c in range(NC - 2, NC):
        for copy in out_copies(c):
            copy.wait()

    ws_remote.wait_send()

    def drain(c, carry):
        for zs in range(Z):
            ref = place(zs, y, rows_all(c))

            @pl.when(has_up & (zs <= z))
            def _(zs=zs, ref=ref):
                along(c, zs, ref, True).wait_send()
                if Y == 2:
                    along_b(c, zs, True).wait_send()

            @pl.when(has_dn & (zs >= z))
            def _(zs=zs, ref=ref):
                along(c, zs, ref, False).wait_send()
                if Y == 2:
                    along_b(c, zs, False).wait_send()

            if Y == 2:
                @pl.when(zs == z)
                def _():
                    across_own(c).wait_send()

                @pl.when(zs != z)
                def _(zs=zs):
                    across(c, zs).wait_send()
        return carry

    lax.fori_loop(0, NC, drain, 0)


def gather_and_multiply(features, weight, shrink_flat, Z, Y):
    rows, depth = features.shape
    width, columns = weight.shape
    T = Z * Y
    CH = rows // CHUNKS
    NB = CH // 6 // 16 * 16
    DMA = pltpu.SemaphoreType.DMA
    per = (CHUNKS, Z)
    few = per if Y == 2 else (1, 1)
    return pl.pallas_call(
        functools.partial(gather_kernel, Z, Y, CH, NB),
        out_shape=(
            jax.ShapeDtypeStruct((rows, columns), jnp.float32),
            jax.ShapeDtypeStruct((rows, 256), jnp.bfloat16),
        ),
        in_specs=[pl.BlockSpec(memory_space=pl.ANY)] * 3,
        out_specs=[pl.BlockSpec(memory_space=pl.ANY)] * 2,
        scratch_shapes=[
            pltpu.VMEM((T, rows, depth), jnp.bfloat16),
            pltpu.VMEM((width, columns), jnp.bfloat16),
            pltpu.VMEM((width, 256), jnp.bfloat16),
            pltpu.VMEM((2, CH, columns), jnp.float32),
            pltpu.VMEM((2, CH, 256), jnp.bfloat16),
            DMA, DMA, DMA, DMA, DMA,
            DMA(per), DMA(per), DMA(per), DMA(few), DMA(few), DMA(few), DMA(few), DMA(few),
            DMA((2, 2)),
        ],
        compiler_params=pltpu.CompilerParams(
            collective_id=0, has_side_effects=True, vmem_limit_bytes=62 * 1024 * 1024,
        ),
        cost_estimate=pl.CostEstimate(
            flops=2 * rows * width * (columns + 256), bytes_accessed=200_000_000, transcendentals=0,
        ),
    )(features, weight, shrink_flat)


def on_device(Z, Y, features, qkv_weight, adapter_ids, owner_slot, shrink_panels, expand_panels):
    rows = features.shape[0]
    columns = qkv_weight.shape[1]
    T = Z * Y
    per_device, width, rank = shrink_panels.shape
    adapter_count = owner_slot.shape[0]
    G = lax.axis_size("groups")
    t = lax.axis_index("tensor")
    slot = slot_of(adapter_ids[:, 0], owner_slot)

    share = rank // G
    mine = lax.dynamic_slice_in_dim(expand_panels, lax.axis_index("groups") * share, share, 1)
    mine = mine.reshape(per_device, share, T, columns).transpose(2, 0, 1, 3)
    got = lax.all_to_all(mine, "tensor", split_axis=0, concat_axis=0, tiled=True)
    panels = lax.all_gather(got, ("rows", "groups"), axis=0, tiled=False)
    panels = panels.reshape(2, G, T, per_device, share, columns).transpose(0, 2, 3, 1, 4, 5)
    panels = panels.reshape(adapter_count * rank, columns)

    shrink_flat = shrink_panels.transpose(1, 0, 2).reshape(width, per_device * rank)
    base, low = gather_and_multiply(features, qkv_weight, shrink_flat, Z, Y)

    held = jnp.arange(2)[:, None] * T * per_device + t * per_device + jnp.arange(per_device)[None, :]
    held = held.reshape(-1).astype(jnp.int32)
    low = low.reshape(rows, 2 * per_device, rank)
    low = jnp.sum(jnp.where((slot[:, None] == held[None, :])[:, :, None], low, 0), axis=1, dtype=jnp.bfloat16)
    shrunk = lax.psum(low, "tensor")
    match = slot[:, None] == jnp.arange(adapter_count, dtype=jnp.int32)[None, :]
    spread = jnp.where(match[:, :, None], shrunk[:, None, :], 0).astype(jnp.bfloat16)
    spread = spread.reshape(rows, adapter_count * rank)
    delta = jnp.dot(spread, panels, preferred_element_type=jnp.float32).astype(jnp.bfloat16)
    return (base + delta.astype(jnp.float32)).astype(jnp.bfloat16)


def solution(mesh):
    Y = max(1, 4 // mesh.shape["groups"])
    Z = mesh.shape["tensor"] // Y
    return jax.shard_map(
        functools.partial(on_device, Z, Y),
        mesh=mesh,
        in_specs=(
            P(("groups", "rows"), "tensor"),
            P(None, "tensor"),
            P(("groups", "rows"), None),
            P(),
            P(("rows", "tensor"), None, None),
            P(("rows", "tensor"), None, None),
        ),
        out_specs=P(("groups", "rows"), "tensor"),
        check_vma=False,
    )
```

time: 1040 us -> 400 us (0.38)
  waiting for transfers between devices: 483 us -> 68.9 us
  blocking collectives: 411 us -> 0 us
  Pallas kernels: 0 us -> 277 us
  local copies, waits for them, and re-layouts: 68.3 us -> 14.1 us
  matrix products: 61.1 us -> 11.7 us
    all_gather x1, waiting for transfers between devices: 482 us -> 0.01 us  [on_device(): panels = lax.all_gather(got, ('rows', 'groups'), axis=0, tiled=False)]
    all_to_all x3 -> x0, blocking collectives: 411 us -> none  [the longest x1 177 us: on_device(): lax.all_to_all(reply, ('rows', 'tensor'), split_axis=0, concat_axis=0, ti...]
    pallas_call x0 -> x1, Pallas kernels: none -> 277 us  [gather_and_multiply(): pl.pallas_call(functools.partial(gather_kernel, Z, Y, CH, NB), out_shape=...]
    psum x0 -> x1, waiting for transfers between devices: none -> 68.9 us  [on_device(): shrunk = lax.psum(low, 'tensor')]
    dot_general x5 -> x1, matrix products: 61.1 us -> 11.7 us  [on_device(): jnp.dot(spread, panels, preferred_element_type=jnp.float32)]
    reshape x3 -> x1, local copies, waits for them, and re-layouts: 33.3 us -> 4.07 us  [on_device(): shrink_panels.transpose(1, 0, 2).reshape(width, per_device * rank)]
    convert_element_type x1 -> x0, local copies, waits for them, and re-layouts: 22.8 us -> none  [on_device(): reply = jnp.einsum('sjmr,jre->sjme', shrunk, expand_panels, preferred_ele...]
    all_to_all x2 -> x0, local copies, waits for them, and re-layouts: 11.2 us -> none  [the longest x1 10.9 us: on_device(): lax.all_to_all(reply, ('rows', 'tensor'), split_axis=0, concat_axis=0, ti...]
  transfers between devices with their start and end apart: 1 -> 3, of which waited for: 1 -> 1; matrix products, arithmetic and copies ran while one was open for 0% -> 3% of each run, Pallas kernels for 0% -> 69%
where the time goes in v1:
time: 400 us; the launch traced here: 399 us
  Pallas kernels  277 us (69%)
  waiting for transfers between devices  68.9 us (17%)
  between operations  14.9 us (4%)
  local copies, waits for them, and re-layouts  14.1 us (4%)
  matrix products  11.7 us (3%)
  starting transfers between devices  7.36 us (2%)
  other arithmetic  5.32 us (1%)
    pallas_call x1, Pallas kernels, gather_and_multiply(): pl.pallas_call(functools.partial(gather_kernel, Z, Y, CH, NB), out_shape=...  277 us
    psum x1, waiting for transfers between devices, on_device(): shrunk = lax.psum(low, 'tensor')  68.9 us
    dot_general x1, matrix products, on_device(): jnp.dot(spread, panels, preferred_element_type=jnp.float32)  11.7 us
  transfers between devices with their start and end apart: 3, of which 1 were waited for; matrix products, arithmetic and copies ran while one was open for 3% of the time, Pallas kernels for 69%

profile of v1, /device:TPU:0, one launch (start us, length us, event | category | flops | bytes accessed | tf_op | source)
XLA Modules:
  0.0 399.3 jit_solution(3871878422997759934)
XLA Ops:
  7.4 1.4 constant_dynamic-slice_fusion
  8.8 0.2 copy.29
  9.0 0.1 bitcast_bitcast_fusion
  9.1 1.4 copy.27
  10.5 7.3 %all-to-all-start = ((bf16[8,2,32,1280]{3,2,1,0:T(8,128)(2,1)}), bf16[8,2,32,1280]{3,2,1,0:T(8,128)(2,1)S(1)}, u32[]{:S(2)}, u32[]{:S(2)}) async-start(bf16[8,2,32,1280]{3,2,1,0:T(8,128)(2,1)} %copy.27), calls=%async_computation | async-start | bytes 2621440 | tf_op jit(solution)/shard_map/all_to_all | solution.py:316
  17.8 0.0 all-reduce.2.cloned.1.call-start
  17.8 4.1 %copy.25.sh_ref = bf16[8192,128]{1,0:T(8,128)(2,1)} copy(bf16[8192,128]{0,1:T(8,128)(2,1)} %bitcast.25) | data formatting | bytes 4194304 | tf_op jit(solution)/shard_map/reshape | solution.py:321
  21.9 0.0 copy-start.2
  21.9 0.0 copy-start.3
  21.9 277.0 %shard_map.64 = (f32[1536,1280]{1,0:T(8,128)}, bf16[1536,256]{1,0:T(8,128)(2,1)}) custom-call(bf16[1536,1024]{1,0:T(8,128)(2,1)} %x_ref.1, bf16[8192,1280]{1,0:T(8,128)(2,1)} %w_ref.1, bf16[8192,128]{1,0:T(8,128)(2,1)} %copy.25.sh_ref), custom_call_target="tpu_custom_call" | custom-call | flops 38654705664 | bytes 200000000 | tf_op jit(solution)/shard_map/pallas_call | solution.py:276
  299.0 0.1 iota_add_fusion
  299.1 0.1 add.44
  299.1 0.0 copy-done.2
  299.2 1.4 copy.26
  300.6 0.0 copy-done.3
  300.6 0.1 select_reduce_fusion.1
  300.7 0.1 broadcast_compare_fusion
  300.8 0.9 select_reduce_fusion
  301.7 0.0 all-reduce.2.cloned.1.call-update
  301.7 0.0 all-gather.3.cloned.1.call-start
  301.7 0.0 all-to-all-done
  301.7 0.0 copy-start.1
  301.8 1.0 copy-done.1
  302.8 0.0 all-gather.3.cloned.1.call-update
  302.9 68.9 %all-reduce.2.cloned.1.call-done = bf16[1536,64]{0,1:T(8,128)(2,1)} async-done(((bf16[1536,64]{0,1:T(8,128)(2,1)}), bf16[1536,64]{0,1:T(8,128)(2,1)}) %all-reduce.2.cloned.1.call-update) | async-done | bytes 196624 | tf_op jit(solution)/shard_map/psum | solution.py:328
  371.8 4.1 %broadcast_select_fusion = bf16[1536,32,64]{0,2,1:T(8,128)(2,1)} fusion(pred[1536,32]{0,1:T(8,128)(4,1)S(1)} %iota_compare_fusion, bf16[1536,64]{0,1:T(8,128)(2,1)} %all-reduce.2.cloned.1.call-done), kind=kLoop, calls=%fused_computation.2 | loop fusion | flops 3145728 | bytes 6537216 | tf_op jit(solution)/shard_map/jit(_where)/select_n | solution.py:330
  375.9 0.0 all-gather.3.cloned.1.call-done
  375.9 0.0 copy-start
  375.9 3.1 copy.28
  379.0 1.3 copy-done
  380.3 11.7 %add_convert_fusion = bf16[1536,1280]{1,0:T(8,128)(2,1)} fusion(f32[1536,1280]{1,0:T(8,128)} %get-tuple-element.7, bf16[1536,2048]{0,1:T(8,128)(2,1)S(1)} %bitcast.19, bf16[2048,1280]{1,0:T(8,128)(2,1)S(1)} %bitcast.21), kind=kOutput, calls=%fused_computation | convolution fusion | flops 8060928000 | bytes 23330816 | tf_op jit(solution)/shard_map/dot_general | solution.py:332
  (3 shorter events, 0.1 us)
Async XLA Ops:
  10.5 291.2 %all-to-all-start = ((bf16[8,2,32,1280]{3,2,1,0:T(8,128)(2,1)}), bf16[8,2,32,1280]{3,2,1,0:T(8,128)(2,1)S(1)}, u32[]{:S(2)}, u32[]{:S(2)}) async-start(bf16[8,2,32,1280]{3,2,1,0:T(8,128)(2,1)} %copy.27), calls=%async_computation | async-start | bytes 2621440 | tf_op jit(solution)/shard_map/all_to_all | solution.py:316
  17.8 354.0 %all-reduce.2.cloned.1.call-start = ((), (), s32[]{:S(2)}) async-start(), calls=%async_computation.1 | async-start | bytes 393216 | tf_op jit(solution)/shard_map/psum | solution.py:328
  21.9 277.2 %copy-start.2 = (s32[1536,1]{0,1:T(1,128)S(1)}, s32[1536,1]{0,1:T(1,128)}, u32[]{:S(2)}) copy-start(s32[1536,1]{0,1:T(1,128)} %param.8) | copy-start | bytes 18436
  21.9 278.7 %copy-start.3 = (s32[32]{0:T(128)S(1)}, s32[32]{0:T(128)}, u32[]{:S(2)}) copy-start(s32[32]{0:T(128)} %param.9) | copy-start | bytes 388
  301.7 74.2 %all-gather.3.cloned.1.call-start = ((), (), s32[]{:S(2)}) async-start(), calls=%async_computation.2 | async-start | bytes 6553600 | tf_op jit(solution)/shard_map/all_gather | solution.py:317
  301.7 1.1 copy-start.1
  375.9 4.3 %copy-start = (bf16[1536,32,64]{0,2,1:T(8,128)(2,1)S(1)}, bf16[1536,32,64]{0,2,1:T(8,128)(2,1)}, u32[]{:S(2)}) copy-start(bf16[1536,32,64]{0,2,1:T(8,128)(2,1)} %broadcast_select_fusion) | copy-start | bytes 18874372
Sparse Core Ops, SparseCore 0:
  301.8 69.9 all-reduce.1
Sparse Core Ops, SparseCore 1:
  303.8 40.2 all-gather.2

commit v2 on v1

--- a/solution.py
+++ b/solution.py
@@ -8,7 +8,7 @@
 from jax.sharding import PartitionSpec as P
 
 CHUNKS = 8
-LAG = 2
+LAG = 1
 
 
 def slot_of(row_ids, owner_slot):
@@ -325,7 +325,14 @@
     held = held.reshape(-1).astype(jnp.int32)
     low = low.reshape(rows, 2 * per_device, rank)
     low = jnp.sum(jnp.where((slot[:, None] == held[None, :])[:, :, None], low, 0), axis=1, dtype=jnp.bfloat16)
-    shrunk = lax.psum(low, "tensor")
+    half = rows // 2
+    low = jnp.concatenate([low[:half], low[half:]], axis=1).reshape(T, half // T, 2 * rank)
+    terms = lax.all_to_all(low, "tensor", split_axis=0, concat_axis=0, tiled=True)
+    part = jnp.sum(terms, axis=0, dtype=jnp.bfloat16)
+    shrunk = lax.all_to_all(
+        jnp.broadcast_to(part[None], terms.shape), "tensor", split_axis=0, concat_axis=0, tiled=True
+    ).reshape(half, 2 * rank)
+    shrunk = jnp.concatenate([shrunk[:, :rank], shrunk[:, rank:]], axis=0)
     match = slot[:, None] == jnp.arange(adapter_count, dtype=jnp.int32)[None, :]
     spread = jnp.where(match[:, :, None], shrunk[:, None, :], 0).astype(jnp.bfloat16)
     spread = spread.reshape(rows, adapter_count * rank)

time: 400 us -> 356 us (0.89)
  waiting for transfers between devices: 68.9 us -> 7.7 us
  blocking collectives: 0 us -> 49.4 us
  Pallas kernels: 277 us -> 255 us
    psum x1 -> x0, waiting for transfers between devices: 68.9 us -> none  [on_device(): shrunk = lax.psum(low, 'tensor')]
    all_to_all x0 -> x2, blocking collectives: none -> 49.4 us  [the longest x1 38.7 us: on_device(): lax.all_to_all(mine, 'tensor', split_axis=0, concat_axis=0, tiled=True)]
    pallas_call x1, Pallas kernels: 277 us -> 255 us  [gather_and_multiply(): pl.pallas_call(functools.partial(gather_kernel, Z, Y, CH, NB), out_shape=...]
    all_to_all x1, waiting for transfers between devices: 0.01 us -> 7.68 us  [on_device(): lax.all_to_all(jnp.broadcast_to(part[None], terms.shape), 'tensor', split...]
  transfers between devices with their start and end apart: 3 -> 2, of which waited for: 1 -> 1; matrix products, arithmetic and copies ran while one was open for 3% -> 3% of each run, Pallas kernels for 69% -> 72%
where the time goes in v2:
time: 356 us
  Pallas kernels  255 us (72%)
  blocking collectives  49.4 us (14%)
  between operations  13.6 us (4%)
  matrix products  11.7 us (3%)
  local copies, waits for them, and re-layouts  11.4 us (3%)
  waiting for transfers between devices  7.7 us (2%)
  other arithmetic  3.85 us (1%)
    pallas_call x1, Pallas kernels, gather_and_multiply(): pl.pallas_call(functools.partial(gather_kernel, Z, Y, CH, NB), out_shape=...  255 us
    all_to_all x1, blocking collectives, on_device(): lax.all_to_all(mine, 'tensor', split_axis=0, concat_axis=0, tiled=True)  38.7 us
    dot_general x1, matrix products, on_device(): jnp.dot(spread, panels, preferred_element_type=jnp.float32)  11.7 us
    all_to_all x1, blocking collectives, on_device(): lax.all_to_all(low, 'tensor', split_axis=0, concat_axis=0, tiled=True)  10.7 us
    all_to_all x1, waiting for transfers between devices, on_device(): lax.all_to_all(jnp.broadcast_to(part[None], terms.shape), 'tensor', split...  7.68 us
  transfers between devices with their start and end apart: 2, of which 1 were waited for; matrix products, arithmetic and copies ran while one was open for 3% of the time, Pallas kernels for 72%

profile of v2, /device:TPU:0, one launch (start us, length us, event | category | flops | bytes accessed | tf_op | source)
XLA Modules:
  0.0 355.5 jit_solution(11496557280587781749)
XLA Ops:
  6.5 0.0 all-gather.3.cloned.1.call-start
  6.5 1.4 constant_dynamic-slice_fusion
  7.9 0.2 copy.42
  8.2 0.0 copy-start.2
  8.2 0.0 copy-start.1
  8.2 0.1 bitcast_bitcast_fusion
  8.3 0.2 copy.40
  8.6 38.7 %all_to_all.15 = bf16[8,2,32,1280]{3,2,1,0:T(8,128)(2,1)} all-to-all(bf16[8,2,32,1280]{3,2,1,0:T(8,128)(2,1)S(1)} %copy.40), channel_id=1, replica_groups=mesh['groups'=2,'rows'=2,'tensor'=8] {'tensor'}, dimensions={0} | all-to-all | bytes 2621440 | tf_op jit(solution)/shard_map/all_to_all | solution.py:316
  47.3 0.0 all-gather.3.cloned.1.call-update
  47.3 0.1 iota_add_fusion
  47.4 0.1 add.42
  47.5 0.0 copy-done.2
  47.5 0.0 copy-done.1
  47.5 2.4 copy.36.sh_ref
  49.9 0.0 copy-start.3
  49.9 254.5 %shard_map.64 = (f32[1536,1280]{1,0:T(8,128)}, bf16[1536,256]{1,0:T(8,128)(2,1)}) custom-call(bf16[1536,1024]{1,0:T(8,128)(2,1)} %x_ref.1, bf16[8192,1280]{1,0:T(8,128)(2,1)} %w_ref.1, bf16[8192,128]{1,0:T(8,128)(2,1)} %copy.36.sh_ref), custom_call_target="tpu_custom_call" | custom-call | flops 38654705664 | bytes 200000000 | tf_op jit(solution)/shard_map/pallas_call | solution.py:276
  304.4 1.4 copy.37
  305.9 0.0 copy-done.3
  305.9 0.1 select_reduce_fusion.1
  306.0 0.1 broadcast_compare_fusion
  306.1 0.2 select_reduce_fusion
  306.3 0.2 copy.38
  306.5 10.7 %all_to_all.16 = bf16[8,96,128]{2,1,0:T(8,128)(2,1)S(1)} all-to-all(bf16[8,96,128]{2,1,0:T(8,128)(2,1)S(1)} %bitcast.29), channel_id=1, replica_groups=mesh['groups'=2,'rows'=2,'tensor'=8] {'tensor'}, dimensions={0} | all-to-all | bytes 393216 | tf_op jit(solution)/shard_map/all_to_all | solution.py:330
  317.2 0.7 broadcast_in_dim.65
  317.9 3.4 all-to-all-start.1
  321.4 7.7 %all-to-all-done.1 = bf16[8,96,128]{2,1,0:T(8,128)(2,1)S(1)} async-done(((bf16[8,96,128]{2,1,0:T(8,128)(2,1)}), bf16[8,96,128]{2,1,0:T(8,128)(2,1)S(1)}, u32[]{:S(2)}, u32[]{:S(2)}) %all-to-all-start.1) | async-done | bytes 196640 | tf_op jit(solution)/shard_map/all_to_all | solution.py:332
  329.1 0.1 fusion
  329.2 0.1 pad_maximum_fusion
  329.3 0.2 copy.39
  329.4 3.2 broadcast_select_fusion
  332.7 0.0 all-gather.3.cloned.1.call-done
  332.7 0.0 copy-start
  332.7 3.1 copy.41
  335.7 1.3 copy-done
  337.0 11.7 %add_convert_fusion = bf16[1536,1280]{1,0:T(8,128)(2,1)} fusion(f32[1536,1280]{1,0:T(8,128)} %get-tuple-element.7, bf16[1536,2048]{0,1:T(8,128)(2,1)S(1)} %bitcast.21, bf16[2048,1280]{1,0:T(8,128)(2,1)S(1)} %bitcast.23), kind=kOutput, calls=%fused_computation | convolution fusion | flops 8060928000 | bytes 23330816 | tf_op jit(solution)/shard_map/dot_general | solution.py:339
  (6 shorter events, 0.1 us)
Async XLA Ops:
  6.5 326.1 %all-gather.3.cloned.1.call-start = ((), (), s32[]{:S(2)}) async-start(), calls=%async_computation.3 | async-start | bytes 6553600 | tf_op jit(solution)/shard_map/all_gather | solution.py:317
  8.2 39.3 %copy-start.2 = (s32[1536,1]{0,1:T(1,128)S(1)}, s32[1536,1]{0,1:T(1,128)}, u32[]{:S(2)}) copy-start(s32[1536,1]{0,1:T(1,128)} %param.8) | copy-start | bytes 18436
  8.2 39.3 %copy-start.1 = (bf16[2,8192,64]{1,2,0:T(8,128)(2,1)S(1)}, bf16[2,8192,64]{1,2,0:T(8,128)(2,1)}, u32[]{:S(2)}) copy-start(bf16[2,8192,64]{1,2,0:T(8,128)(2,1)} %param.10) | copy-start | bytes 6291460
  49.9 255.9 %copy-start.3 = (s32[32]{0:T(128)S(1)}, s32[32]{0:T(128)}, u32[]{:S(2)}) copy-start(s32[32]{0:T(128)} %param.9) | copy-start | bytes 388
  317.9 11.1 %all-to-all-start.1 = ((bf16[8,96,128]{2,1,0:T(8,128)(2,1)}), bf16[8,96,128]{2,1,0:T(8,128)(2,1)S(1)}, u32[]{:S(2)}, u32[]{:S(2)}) async-start(bf16[8,96,128]{2,1,0:T(8,128)(2,1)} %broadcast_in_dim.65), calls=%async_computation.1 | async-start | bytes 393216 | tf_op jit(solution)/shard_map/all_to_all | solution.py:332
  332.7 4.3 %copy-start = (bf16[1536,32,64]{0,2,1:T(8,128)(2,1)S(1)}, bf16[1536,32,64]{0,2,1:T(8,128)(2,1)}, u32[]{:S(2)}) copy-start(bf16[1536,32,64]{0,2,1:T(8,128)(2,1)} %broadcast_select_fusion) | copy-start | bytes 18874372
Sparse Core Ops, SparseCore 0:
  47.4 39.4 all-gather.2

commit v3 on v2

--- a/solution.py
+++ b/solution.py
@@ -18,9 +18,10 @@
 
 
 def gather_kernel(
-    Z, Y, CH, NB,
-    x_ref, w_ref, sh_ref, base_ref, low_ref,
+    Z, Y, G, CH, NB,
+    x_ref, w_ref, sh_ref, cut_ref, base_ref, low_ref, e_ref,
     g, w, ws, acc, low,
+    e_sem, e_send, e_recv, p_send, p_recv,
     own_sem, w_sem, ws_sem, ws_send, ws_recv,
     up_send, dn_send, z_recv, ub_send, db_send, b_recv, y_send, y_recv, out_sem,
 ):
@@ -37,18 +38,47 @@
 
     barrier = pltpu.get_barrier_semaphore()
 
-    @pl.when(has_up)
-    def _():
-        pl.semaphore_signal(barrier, inc=1, device_id=up)
-
-    @pl.when(has_dn)
-    def _():
-        pl.semaphore_signal(barrier, inc=1, device_id=dn)
-
-    if Y == 2:
-        pl.semaphore_signal(barrier, inc=1, device_id=side)
-    pl.semaphore_signal(barrier, inc=1, device_id=twin)
-    pl.semaphore_wait(barrier, has_up.astype(jnp.int32) + has_dn.astype(jnp.int32) + Y)
+    for d in range(1, T):
+        pl.semaphore_signal(barrier, inc=1, device_id={"tensor": lax.rem(t + d, T)})
+    peers = 2 * G
+    group = lax.axis_index("groups")
+    at = r * G + group
+
+    def peer(e):
+        p = lax.rem(at + e, peers)
+        return {"rows": p // G, "groups": lax.rem(p, G)}
+
+    for e in range(1, peers):
+        pl.semaphore_signal(barrier, inc=1, device_id=peer(e))
+    pl.semaphore_wait(barrier, T - 1 + peers - 1)
+
+    e_own = pltpu.make_async_copy(cut_ref.at[t], e_ref.at[at, t], e_sem)
+
+    def e_out(d):
+        to = lax.rem(t + d, T)
+        return pltpu.make_async_remote_copy(
+            src_ref=cut_ref.at[to], dst_ref=e_ref.at[at, t],
+            send_sem=e_send.at[d], recv_sem=e_recv.at[d], device_id={"tensor": to},
+        )
+
+    def e_in(d):
+        return pltpu.make_async_remote_copy(
+            src_ref=cut_ref.at[t], dst_ref=e_ref.at[at, lax.rem(t + T - d, T)],
+            send_sem=e_send.at[d], recv_sem=e_recv.at[d], device_id={"tensor": lax.rem(t + d, T)},
+        )
+
+    def p_out(e):
+        return pltpu.make_async_remote_copy(
+            src_ref=e_ref.at[at], dst_ref=e_ref.at[at],
+            send_sem=p_send.at[e], recv_sem=p_recv.at[e], device_id=peer(e),
+        )
+
+    def p_in(e):
+        ref = e_ref.at[lax.rem(at + peers - e, peers)]
+        return pltpu.make_async_remote_copy(
+            src_ref=ref, dst_ref=ref,
+            send_sem=p_send.at[e], recv_sem=p_recv.at[e], device_id=peer(e),
+        )
 
     own_copy = pltpu.make_async_copy(x_ref, g.at[t], own_sem)
     w_copy = pltpu.make_async_copy(w_ref, w, w_sem)
@@ -161,6 +191,17 @@
             ws_copy.start()
             own_copy.start()
             w_copy.start()
+            e_own.start()
+            for d in range(1, T):
+                e_out(d).start()
+
+        @pl.when(k == Z)
+        def _():
+            e_own.wait()
+            for d in range(1, T):
+                e_in(d).wait_recv()
+            for e in range(1, peers):
+                p_out(e).start()
 
         if Y == 2:
             c1 = k - LAG
@@ -234,6 +275,11 @@
             copy.wait()
 
     ws_remote.wait_send()
+    for d in range(1, T):
+        e_out(d).wait_send()
+    for e in range(1, peers):
+        p_out(e).wait_send()
+        p_in(e).wait_recv()
 
     def drain(c, carry):
         for zs in range(Z):
@@ -264,7 +310,7 @@
     lax.fori_loop(0, NC, drain, 0)
 
 
-def gather_and_multiply(features, weight, shrink_flat, Z, Y):
+def gather_and_multiply(features, weight, shrink_flat, cut, Z, Y, G):
     rows, depth = features.shape
     width, columns = weight.shape
     T = Z * Y
@@ -274,19 +320,21 @@
     per = (CHUNKS, Z)
     few = per if Y == 2 else (1, 1)
     return pl.pallas_call(
-        functools.partial(gather_kernel, Z, Y, CH, NB),
+        functools.partial(gather_kernel, Z, Y, G, CH, NB),
         out_shape=(
             jax.ShapeDtypeStruct((rows, columns), jnp.float32),
             jax.ShapeDtypeStruct((rows, 256), jnp.bfloat16),
+            jax.ShapeDtypeStruct((2 * G,) + cut.shape, jnp.bfloat16),
         ),
-        in_specs=[pl.BlockSpec(memory_space=pl.ANY)] * 3,
-        out_specs=[pl.BlockSpec(memory_space=pl.ANY)] * 2,
+        in_specs=[pl.BlockSpec(memory_space=pl.ANY)] * 4,
+        out_specs=[pl.BlockSpec(memory_space=pl.ANY)] * 3,
         scratch_shapes=[
             pltpu.VMEM((T, rows, depth), jnp.bfloat16),
             pltpu.VMEM((width, columns), jnp.bfloat16),
             pltpu.VMEM((width, 256), jnp.bfloat16),
             pltpu.VMEM((2, CH, columns), jnp.float32),
             pltpu.VMEM((2, CH, 256), jnp.bfloat16),
+            DMA, DMA((T,)), DMA((T,)), DMA((2 * G,)), DMA((2 * G,)),
             DMA, DMA, DMA, DMA, DMA,
             DMA(per), DMA(per), DMA(per), DMA(few), DMA(few), DMA(few), DMA(few), DMA(few),
             DMA((2, 2)),
@@ -297,7 +345,7 @@
         cost_estimate=pl.CostEstimate(
             flops=2 * rows * width * (columns + 256), bytes_accessed=200_000_000, transcendentals=0,
         ),
-    )(features, weight, shrink_flat)
+    )(features, weight, shrink_flat, cut)
 
 
 def on_device(Z, Y, features, qkv_weight, adapter_ids, owner_slot, shrink_panels, expand_panels):
@@ -312,14 +360,10 @@
 
     share = rank // G
     mine = lax.dynamic_slice_in_dim(expand_panels, lax.axis_index("groups") * share, share, 1)
-    mine = mine.reshape(per_device, share, T, columns).transpose(2, 0, 1, 3)
-    got = lax.all_to_all(mine, "tensor", split_axis=0, concat_axis=0, tiled=True)
-    panels = lax.all_gather(got, ("rows", "groups"), axis=0, tiled=False)
-    panels = panels.reshape(2, G, T, per_device, share, columns).transpose(0, 2, 3, 1, 4, 5)
+    cut = mine.reshape(per_device * share, T, columns).transpose(1, 0, 2)
+    shrink_flat = shrink_panels.transpose(1, 0, 2).reshape(width, per_device * rank)
+    base, low, panels = gather_and_multiply(features, qkv_weight, shrink_flat, cut, Z, Y, G)
     panels = panels.reshape(adapter_count * rank, columns)
-
-    shrink_flat = shrink_panels.transpose(1, 0, 2).reshape(width, per_device * rank)
-    base, low = gather_and_multiply(features, qkv_weight, shrink_flat, Z, Y)
 
     held = jnp.arange(2)[:, None] * T * per_device + t * per_device + jnp.arange(per_device)[None, :]
     held = held.reshape(-1).astype(jnp.int32)
@@ -333,8 +377,9 @@
         jnp.broadcast_to(part[None], terms.shape), "tensor", split_axis=0, concat_axis=0, tiled=True
     ).reshape(half, 2 * rank)
     shrunk = jnp.concatenate([shrunk[:, :rank], shrunk[:, rank:]], axis=0)
-    match = slot[:, None] == jnp.arange(adapter_count, dtype=jnp.int32)[None, :]
-    spread = jnp.where(match[:, :, None], shrunk[:, None, :], 0).astype(jnp.bfloat16)
+    match = (slot[:, None] == jnp.arange(adapter_count, dtype=jnp.int32)[None, :])
+    match = match.reshape(rows, 2, 1, T * per_device, 1)
+    spread = jnp.where(match, shrunk.reshape(rows, 1, G, 1, share), 0).astype(jnp.bfloat16)
     spread = spread.reshape(rows, adapter_count * rank)
     delta = jnp.dot(spread, panels, preferred_element_type=jnp.float32).astype(jnp.bfloat16)
     return (base + delta.astype(jnp.float32)).astype(jnp.bfloat16)

time: 356 us -> 327 us (0.919)
  blocking collectives: 49.4 us -> 0 us
  Pallas kernels: 255 us -> 280 us
  between operations: 13.6 us -> 0.12 us
  waiting for transfers between devices: 7.7 us -> 15.3 us
    all_to_all x2 -> x0, blocking collectives: 49.4 us -> none  [the longest x1 38.7 us: on_device(): lax.all_to_all(mine, 'tensor', split_axis=0, concat_axis=0, tiled=True)]
    pallas_call x1, Pallas kernels: 255 us -> 280 us  [gather_and_multiply(): pl.pallas_call(functools.partial(gather_kernel, Z, Y, G, CH, NB), out_sha...]
    all_to_all x0 -> x1, waiting for transfers between devices: none -> 7.71 us  [on_device(): lax.all_to_all(low, 'tensor', split_axis=0, concat_axis=0, tiled=True)]
  transfers between devices with their start and end apart: 2 -> 2, of which waited for: 1 -> 2; matrix products, arithmetic and copies ran while one was open for 3% -> 0% of each run, Pallas kernels for 72% -> 0%
where the time goes in v3:
time: 327 us
  Pallas kernels  280 us (86%)
  waiting for transfers between devices  15.3 us (5%)
  matrix products  11.7 us (4%)
  local copies, waits for them, and re-layouts  10.5 us (3%)
  starting transfers between devices  6.78 us (2%)
    pallas_call x1, Pallas kernels, gather_and_multiply(): pl.pallas_call(functools.partial(gather_kernel, Z, Y, G, CH, NB), out_sha...  280 us
    dot_general x1, matrix products, on_device(): jnp.dot(spread, panels, preferred_element_type=jnp.float32)  11.7 us
    all_to_all x1, waiting for transfers between devices, on_device(): lax.all_to_all(low, 'tensor', split_axis=0, concat_axis=0, tiled=True)  7.71 us
    all_to_all x1, waiting for transfers between devices, on_device(): lax.all_to_all(jnp.broadcast_to(part[None], terms.shape), 'tensor', split...  7.62 us
  transfers between devices with their start and end apart: 2, of which 2 were waited for; matrix products, arithmetic and copies ran while one was open for 0% of the time, Pallas kernels for 0%

profile of v3, /device:TPU:0, one launch (start us, length us, event | category | flops | bytes accessed | tf_op | source)
XLA Modules:
  0.0 327.0 jit_solution(13318614858746468863)
XLA Ops:
  0.0 0.0 copy-start
  0.0 0.1 iota_add_fusion
  0.1 0.1 add.48
  0.2 0.8 reduce
  1.0 1.4 constant_dynamic-slice_fusion
  2.4 0.2 copy.29
  2.7 1.3 copy.31
  3.9 0.0 copy-done
  3.9 2.4 copy.25.sh_ref
  6.4 0.0 copy-start.1
  6.4 280.5 %shard_map.64 = (f32[1536,1280]{1,0:T(8,128)}, bf16[1536,256]{1,0:T(8,128)(2,1)}, bf16[4,8,64,1280]{3,2,1,0:T(8,128)(2,1)}) custom-call(bf16[1536,1024]{1,0:T(8,128)(2,1)} %x_ref.1, bf16[8192,1280]{1,0:T(8,128)(2,1)} %w_ref.1, bf16[8192,128]{1,0:T(8,128)(2,1)} %copy.25.sh_ref, bf16[8,64,1280]{2,1,0:T(8,128)(2,1)} %bitcast.23), custom_call_target="tpu_custom_call" | custom-call | flops 38654705664 | bytes 200000000 | tf_op jit(solution)/shard_map/pallas_call | solution.py:322
  286.8 1.4 copy.26
  288.3 0.0 copy-done.1
  288.3 0.1 select_reduce_fusion.1
  288.4 0.1 broadcast_compare_fusion.1
  288.5 0.2 select_reduce_fusion
  288.7 0.8 copy.27
  289.5 3.4 %all-to-all-start = ((bf16[8,96,128]{2,1,0:T(8,128)(2,1)}), bf16[8,96,128]{2,1,0:T(8,128)(2,1)S(1)}, u32[]{:S(2)}, u32[]{:S(2)}) async-start(bf16[8,96,128]{2,1,0:T(8,128)(2,1)} %bitcast.4), calls=%async_computation | async-start | bytes 393216 | tf_op jit(solution)/shard_map/all_to_all | solution.py:374
  292.9 7.7 %all-to-all-done = bf16[8,96,128]{2,1,0:T(8,128)(2,1)S(1)} async-done(((bf16[8,96,128]{2,1,0:T(8,128)(2,1)}), bf16[8,96,128]{2,1,0:T(8,128)(2,1)S(1)}, u32[]{:S(2)}, u32[]{:S(2)}) %all-to-all-start) | async-done | bytes 196640 | tf_op jit(solution)/shard_map/all_to_all | solution.py:374
  300.7 0.7 broadcast_in_dim.65
  301.4 3.4 %all-to-all-start.1 = ((bf16[8,96,128]{2,1,0:T(8,128)(2,1)}), bf16[8,96,128]{2,1,0:T(8,128)(2,1)S(1)}, u32[]{:S(2)}, u32[]{:S(2)}) async-start(bf16[8,96,128]{2,1,0:T(8,128)(2,1)} %broadcast_in_dim.65), calls=%async_computation.1 | async-start | bytes 393216 | tf_op jit(solution)/shard_map/all_to_all | solution.py:376
  304.8 0.1 broadcast_compare_fusion
  304.9 7.6 %all-to-all-done.1 = bf16[8,96,128]{2,1,0:T(8,128)(2,1)S(1)} async-done(((bf16[8,96,128]{2,1,0:T(8,128)(2,1)}), bf16[8,96,128]{2,1,0:T(8,128)(2,1)S(1)}, u32[]{:S(2)}, u32[]{:S(2)}) %all-to-all-start.1) | async-done | bytes 196640 | tf_op jit(solution)/shard_map/all_to_all | solution.py:376
  312.5 0.1 fusion
  312.6 0.1 pad_maximum_fusion
  312.7 0.2 copy.28
  312.9 0.0 copy-start.2
  312.9 0.6 broadcast_select_fusion
  313.5 1.8 copy-done.2
  315.4 11.7 %add_convert_fusion = bf16[1536,1280]{1,0:T(8,128)(2,1)} fusion(f32[1536,1280]{1,0:T(8,128)} %get-tuple-element.8, bf16[1536,2048]{0,1:T(8,128)(2,1)S(1)} %bitcast.17, bf16[2048,1280]{1,0:T(8,128)(2,1)S(1)} %bitcast.25), kind=kOutput, calls=%fused_computation | convolution fusion | flops 8060928000 | bytes 23330816 | tf_op jit(solution)/shard_map/dot_general | solution.py:384
  (5 shorter events, 0.1 us)
Async XLA Ops:
  0.0 3.9 %copy-start = (bf16[2,8192,64]{1,2,0:T(8,128)(2,1)S(1)}, bf16[2,8192,64]{1,2,0:T(8,128)(2,1)}, u32[]{:S(2)}) copy-start(bf16[2,8192,64]{1,2,0:T(8,128)(2,1)} %param.10) | copy-start | bytes 6291460
  6.4 281.9 %copy-start.1 = (s32[32]{0:T(128)S(1)}, s32[32]{0:T(128)}, u32[]{:S(2)}) copy-start(s32[32]{0:T(128)} %param.9) | copy-start | bytes 388
  289.5 11.1 %all-to-all-start = ((bf16[8,96,128]{2,1,0:T(8,128)(2,1)}), bf16[8,96,128]{2,1,0:T(8,128)(2,1)S(1)}, u32[]{:S(2)}, u32[]{:S(2)}) async-start(bf16[8,96,128]{2,1,0:T(8,128)(2,1)} %bitcast.4), calls=%async_computation | async-start | bytes 393216 | tf_op jit(solution)/shard_map/all_to_all | solution.py:374
  301.4 11.1 %all-to-all-start.1 = ((bf16[8,96,128]{2,1,0:T(8,128)(2,1)}), bf16[8,96,128]{2,1,0:T(8,128)(2,1)S(1)}, u32[]{:S(2)}, u32[]{:S(2)}) async-start(bf16[8,96,128]{2,1,0:T(8,128)(2,1)} %broadcast_in_dim.65), calls=%async_computation.1 | async-start | bytes 393216 | tf_op jit(solution)/shard_map/all_to_all | solution.py:376
  312.9 2.5 copy-start.2
